TPU v7x, 128 devices: a whole 4x4x4 slice. The times are simulated.
128 devices in a mesh: rollout: 16 (over y, x_hi, core), tp: 8 (over z, x_lo).
Axes of the slice: x: 4 (x_hi: 2, x_lo: 2; x = x_hi * 2 + x_lo), y: 4, z: 4, core: 2. Of those that a mesh axis runs over, the one named last changes fastest.
Arguments:
- tokens: bfloat16 [4096, 8192], P('rollout'), may hold values from -800 to 800
- norm_gain: float32 [8192], replicated, may hold values from 0.5 to 1.5
- query_weight: bfloat16 [8192, 8192], P(None, 'tp'), may hold values from -0.0625 to 0.0625
- key_matrix: bfloat16 [8192, 1024], P(None, 'tp'), may hold values from -0.25 to 0.25
- value_matrix: bfloat16 [8192, 1024], P(None, 'tp'), may hold values from -0.0625 to 0.0625
- prompt_cache: bfloat16 [2, 16384, 8, 128], P(None, ('rollout', 'tp')), may hold values from -330 to 330
- lengths: int32 [16], P('rollout'), may hold values from 128 to 256, as said below
Outputs:
- context: bfloat16 [4096, 8192], P('rollout', 'tp')
Inputs may be any that keep to these rules, and one draw needn't show every extreme that they name: `lengths`: each length is a multiple of 128.
All inputs are finite; a program needn't handle non-finite values.
Results may differ from a plain program's by a relative error of at most 0.022.
Values may be sent and summed in bfloat16 or wider, within the bound.
A program may use at most 320 MiB of HBM per device.

v0:
```python
import jax
import jax.numpy as jnp
from jax import lax
from jax.sharding import PartitionSpec as P

HEAD_SIZE = 128


rope_base = 500000.0


def rotary_apply(values, token_position):
    half_width = values.shape[-1] // 2
    frequency = jnp.power(
        jnp.float32(rope_base), -2.0 * jnp.arange(half_width, dtype=jnp.float32) / values.shape[-1]
    )
    angles = token_position[:, None] * frequency[None, :]
    cos_shape = (values.shape[0],) + (1,) * (values.ndim - 2) + (half_width,)
    cosine = jnp.cos(angles).reshape(cos_shape)
    sine_part = jnp.sin(angles).reshape(cos_shape)
    lower_half = values[..., :half_width]
    upper_half = values[..., half_width:]
    return jnp.concatenate(
        [
            lower_half * cosine - upper_half * sine_part,
            upper_half * cosine + lower_half * sine_part,
        ],
        axis=-1,
    )


def update(carry, scores, values):
    row_max, row_sum, accum = carry
    new_max = jnp.maximum(row_max, scores.max(axis=-1))
    factor = jnp.exp(row_max - new_max)
    weights = jnp.exp(scores - new_max[..., None])
    row_sum = row_sum * factor + weights.sum(axis=-1)
    accum = accum * factor[..., None] + jnp.einsum(
        "rgqk,kgd->rgqd", weights.astype(jnp.bfloat16), values, preferred_element_type=jnp.float32
    )
    return (new_max, row_sum, accum)


def shards(tokens, norm_gain, query_weight, key_matrix, value_matrix, prompt_cache, lengths):
    count_of_rows = tokens.shape[0]
    kv_local = key_matrix.shape[1] // HEAD_SIZE
    query_group_size = query_weight.shape[1] // key_matrix.shape[1]
    prompt_length = prompt_cache.shape[1] * lax.axis_size("rollout") * lax.axis_size("tp")
    score_scale = HEAD_SIZE ** (-0.5)
    widened = tokens.astype(jnp.float32)
    normalized_input = (
        widened * lax.rsqrt(jnp.mean(widened * widened, axis=-1, keepdims=True) + 1e-05) * norm_gain
    ).astype(jnp.bfloat16)
    token_position = (prompt_length + jnp.arange(count_of_rows)).astype(jnp.float32)
    query_matrix = rotary_apply(
        jnp.dot(normalized_input, query_weight, preferred_element_type=jnp.float32).reshape(
            count_of_rows, kv_local * query_group_size, HEAD_SIZE
        ),
        token_position,
    )
    query_matrix = query_matrix.astype(jnp.bfloat16).reshape(
        count_of_rows, kv_local, query_group_size, HEAD_SIZE
    )
    fresh_key = rotary_apply(
        jnp.dot(normalized_input, key_matrix, preferred_element_type=jnp.float32).reshape(
            count_of_rows, kv_local, HEAD_SIZE
        ),
        token_position,
    ).astype(jnp.bfloat16)
    fresh_value = (
        jnp.dot(normalized_input, value_matrix, preferred_element_type=jnp.float32)
        .astype(jnp.bfloat16)
        .reshape(count_of_rows, kv_local, HEAD_SIZE)
    )

    def absorb(carry, piece):
        scores = (
            jnp.einsum("rgqd,kgd->rgqk", query_matrix, piece[0], preferred_element_type=jnp.float32)
            * score_scale
        )
        return update(carry, scores, piece[1])

    initial = (
        jnp.full((count_of_rows, kv_local, query_group_size), -1e30, jnp.float32),
        jnp.zeros((count_of_rows, kv_local, query_group_size), jnp.float32),
        jnp.zeros((count_of_rows, kv_local, query_group_size, HEAD_SIZE), jnp.float32),
    )
    gathered = lax.all_gather(prompt_cache, "rollout", axis=1, tiled=True)
    regrouped = lax.all_to_all(gathered, "tp", split_axis=2, concat_axis=1, tiled=True)
    span = regrouped.shape[1] // lax.axis_size("tp")

    def sweep(step, carry_now):
        piece = lax.dynamic_slice_in_dim(regrouped, step * span, span, 1)
        return absorb(carry_now, piece)

    carry = lax.fori_loop(0, lax.axis_size("tp"), sweep, initial)
    near_scores = (
        jnp.einsum("rgqd,ugd->rgqu", query_matrix, fresh_key, preferred_element_type=jnp.float32)
        * score_scale
    )
    causal = jnp.arange(count_of_rows)[None, :] <= jnp.arange(count_of_rows)[:, None]
    near_scores = jnp.where(causal[:, None, None, :], near_scores, -jnp.inf)
    row_max, row_sum, accum = update(carry, near_scores, fresh_value)
    result = accum / row_sum[..., None]
    live_rows = jnp.arange(count_of_rows) < lengths[0]
    result = jnp.where(live_rows[:, None, None, None], result, 0.0).astype(jnp.bfloat16)
    return result.reshape(count_of_rows, kv_local * query_group_size * HEAD_SIZE)


def solution(mesh):
    placed = (
        P("rollout", None),
        P(),
        P(None, "tp"),
        P(None, "tp"),
        P(None, "tp"),
        P(None, ("rollout", "tp"), None, None),
        P("rollout"),
    )
    return jax.shard_map(
        shards, mesh=mesh, in_specs=placed, out_specs=P("rollout", "tp"), check_vma=False
    )
```

profile of v0, /device:TPU:0, one launch (start us, length us, event | category | flops | bytes accessed | tf_op | source)
XLA Modules:
  0.0 418.2 jit_solution(13079099454091215464)
XLA Ops:
  6.5 2.1 copy.26
  8.7 76.5 %all-gather.2.cloned.1.call-done = bf16[2,2048,8,128]{3,1,0,2:T(8,128)(2,1)} async-done(((bf16[2,128,8,128]{3,1,0,2:T(8,128)(2,1)}), bf16[2,2048,8,128]{3,1,0,2:T(8,128)(2,1)}) %all-gather.2.cloned.1.call-update) | async-done | bytes 8388624 | tf_op jit(solution)/shard_map/all_gather | solution.py:88
  85.2 4.9 %all-to-all-start = ((bf16[2,2048,8,128]{3,1,0,2:T(8,128)(2,1)}), bf16[2,2048,8,128]{3,1,0,2:T(8,128)(2,1)}, u32[]{:S(2)}, u32[]{:S(2)}) async-start(bf16[2,2048,8,128]{3,1,0,2:T(8,128)(2,1)} %all-gather.2.cloned.1.call-done), calls=%async_computation | async-start | bytes 16777216 | tf_op jit(solution)/shard_map/all_to_all | solution.py:89
  90.8 3.1 fusion.18
  93.9 9.6 %convolution_bitcast_fusion = f32[32,8,8,128]{3,1,2,0:T(8,128)S(1)} fusion(bf16[8192,1024]{1,0:T(8,128)(2,1)} %param.11, bf16[256,8192]{1,0:T(8,128)(2,1)} %param.9, f32[8192]{0:T(1024)S(1)} %copy-done.5, f32[256]{0:T(256)S(1)} %add_rsqrt_fusion), kind=kOutput, calls=%fused_computation.31 | convolution fusion | flops 4303355904 | bytes 22053888 | tf_op jit(solution)/shard_map/dot_general | solution.py:56
  103.8 0.5 multiply_cosine_fusion
  104.7 0.4 subtract_convert_fusion
  105.7 0.7 copy-done.4
  106.4 1.7 convolution_bitcast_fusion.2
  108.4 2.0 fusion.55
  110.5 74.8 %all-to-all-done = bf16[2,2048,8,128]{3,1,0,2:T(8,128)(2,1)} async-done(((bf16[2,2048,8,128]{3,1,0,2:T(8,128)(2,1)}), bf16[2,2048,8,128]{3,1,0,2:T(8,128)(2,1)}, u32[]{:S(2)}, u32[]{:S(2)}) %all-to-all-start) | async-done | bytes 8388640 | tf_op jit(solution)/shard_map/all_to_all | solution.py:89
  185.3 7.4 %copy.27 = bf16[2,2048,8,128]{3,1,2,0:T(8,128)(2,1)} copy(bf16[2,2048,8,128]{3,1,0,2:T(8,128)(2,1)} %all-to-all-done) | data formatting | bytes 16777216 | tf_op jit(solution)/shard_map/all_to_all | solution.py:89
  192.7 210.9 %while.18 = (s32[]{:T(128)}, f32[256,1,8]{0,2,1:T(8,128)S(1)}, f32[256,1,8]{0,2,1:T(8,128)S(1)}, f32[256,1,8,128]{0,3,2,1:T(8,128)}, bf16[2,16384,1,128]{3,1,2,0...) while((s32[]{:T(128)}, f32[256,1,8]{0,2,1:T(8,128)S(1)}, ...), condition=%wide.region_4.0_spmd.clone, body=%wide.region_1.0_spmd.clone.sunk | while | flops 2181836800 | bytes 62521596 | solution.py:96
  192.7 9.1 %bitcast_reduce_fusion.2 = (f32[256,8]{0,1:T(8,128)S(1)}, f32[2048,256,8]{1,0,2:T(8,128)}) fusion(bf16[256,1,8,128]{3,0,2,1:T(8,128)(2,1)S(1)} %get-tuple-element.246, bf16[2,16384,1,128]{3,1,2,0:T(8,128)(2,1)} %get-tuple-element.245, s32[]{:T(128)S(6)} %select_n.23), kind=kOutput, calls=%fused_computation.1.clone.1 | convolution fusion | flops 1082128384 | bytes 17833988 | tf_op jit(solution)/shard_map/while/body/eval_jaxpr/rgqd,kgd->rgqk/dot_general | solution.py:78
  201.8 8.6 %fusion.65 = f32[256,8]{0,1:T(8,128)S(1)} fusion(f32[2048,256,8]{1,0,2:T(8,128)} %get-tuple-element.217, f32[256,8]{0,1:T(8,128)S(1)} %bitcast.152), kind=kLoop, calls=%fused_computation.4.clone.1 | loop fusion | flops 12580864 | bytes 16793600 | tf_op jit(solution)/shard_map/while/body/eval_jaxpr/reduce_sum | solution.py:37
  210.4 7.6 %fusion.66 = f32[256,1,8,128]{0,3,2,1:T(8,128)S(1)} fusion(f32[2048,256,8]{1,0,2:T(8,128)} %get-tuple-element.217, f32[256,8]{0,1:T(8,128)S(1)} %bitcast.153, f32[256,1,8,128]{0,3,2,1:T(8,128)S(1)} %copy-done.1, bf16[2,16384,1,128]{3,1,2,0:T(8,128)(2,1)} %get-tuple-element.245, s32[]{:T(128)S(6)} %add.128, s32[]{:T(128)S(6)} %select_n.23, ...), kind=kOutput, calls=%fused_computation.8.clone.1 | convolution fusion | flops 1087111168 | bytes 19415048 | tf_op jit(solution)/shard_map/while/body/eval_jaxpr/rgqk,kgd->rgqd/dot_general | solution.py:38
  218.1 0.9 copy-done.2
  219.0 9.1 %bitcast_reduce_fusion.2 = (f32[256,8]{0,1:T(8,128)S(1)}, f32[2048,256,8]{1,0,2:T(8,128)}) fusion(bf16[256,1,8,128]{3,0,2,1:T(8,128)(2,1)S(1)} %get-tuple-element.246, bf16[2,16384,1,128]{3,1,2,0:T(8,128)(2,1)} %get-tuple-element.245, s32[]{:T(128)S(6)} %select_n.23), kind=kOutput, calls=%fused_computation.1.clone.1 | convolution fusion | flops 1082128384 | bytes 17833988 | tf_op jit(solution)/shard_map/while/body/eval_jaxpr/rgqd,kgd->rgqk/dot_general | solution.py:78
  228.1 8.6 %fusion.65 = f32[256,8]{0,1:T(8,128)S(1)} fusion(f32[2048,256,8]{1,0,2:T(8,128)} %get-tuple-element.217, f32[256,8]{0,1:T(8,128)S(1)} %bitcast.152), kind=kLoop, calls=%fused_computation.4.clone.1 | loop fusion | flops 12580864 | bytes 16793600 | tf_op jit(solution)/shard_map/while/body/eval_jaxpr/reduce_sum | solution.py:37
  236.8 7.6 %fusion.66 = f32[256,1,8,128]{0,3,2,1:T(8,128)S(1)} fusion(f32[2048,256,8]{1,0,2:T(8,128)} %get-tuple-element.217, f32[256,8]{0,1:T(8,128)S(1)} %bitcast.153, f32[256,1,8,128]{0,3,2,1:T(8,128)S(1)} %copy-done.1, bf16[2,16384,1,128]{3,1,2,0:T(8,128)(2,1)} %get-tuple-element.245, s32[]{:T(128)S(6)} %add.128, s32[]{:T(128)S(6)} %select_n.23, ...), kind=kOutput, calls=%fused_computation.8.clone.1 | convolution fusion | flops 1087111168 | bytes 19415048 | tf_op jit(solution)/shard_map/while/body/eval_jaxpr/rgqk,kgd->rgqd/dot_general | solution.py:38
  244.5 0.9 copy-done.2
  245.4 9.1 %bitcast_reduce_fusion.2 = (f32[256,8]{0,1:T(8,128)S(1)}, f32[2048,256,8]{1,0,2:T(8,128)}) fusion(bf16[256,1,8,128]{3,0,2,1:T(8,128)(2,1)S(1)} %get-tuple-element.246, bf16[2,16384,1,128]{3,1,2,0:T(8,128)(2,1)} %get-tuple-element.245, s32[]{:T(128)S(6)} %select_n.23), kind=kOutput, calls=%fused_computation.1.clone.1 | convolution fusion | flops 1082128384 | bytes 17833988 | tf_op jit(solution)/shard_map/while/body/eval_jaxpr/rgqd,kgd->rgqk/dot_general | solution.py:78
  254.5 8.6 %fusion.65 = f32[256,8]{0,1:T(8,128)S(1)} fusion(f32[2048,256,8]{1,0,2:T(8,128)} %get-tuple-element.217, f32[256,8]{0,1:T(8,128)S(1)} %bitcast.152), kind=kLoop, calls=%fused_computation.4.clone.1 | loop fusion | flops 12580864 | bytes 16793600 | tf_op jit(solution)/shard_map/while/body/eval_jaxpr/reduce_sum | solution.py:37
  263.1 7.6 %fusion.66 = f32[256,1,8,128]{0,3,2,1:T(8,128)S(1)} fusion(f32[2048,256,8]{1,0,2:T(8,128)} %get-tuple-element.217, f32[256,8]{0,1:T(8,128)S(1)} %bitcast.153, f32[256,1,8,128]{0,3,2,1:T(8,128)S(1)} %copy-done.1, bf16[2,16384,1,128]{3,1,2,0:T(8,128)(2,1)} %get-tuple-element.245, s32[]{:T(128)S(6)} %add.128, s32[]{:T(128)S(6)} %select_n.23, ...), kind=kOutput, calls=%fused_computation.8.clone.1 | convolution fusion | flops 1087111168 | bytes 19415048 | tf_op jit(solution)/shard_map/while/body/eval_jaxpr/rgqk,kgd->rgqd/dot_general | solution.py:38
  270.8 0.9 copy-done.2
  271.7 9.1 %bitcast_reduce_fusion.2 = (f32[256,8]{0,1:T(8,128)S(1)}, f32[2048,256,8]{1,0,2:T(8,128)}) fusion(bf16[256,1,8,128]{3,0,2,1:T(8,128)(2,1)S(1)} %get-tuple-element.246, bf16[2,16384,1,128]{3,1,2,0:T(8,128)(2,1)} %get-tuple-element.245, s32[]{:T(128)S(6)} %select_n.23), kind=kOutput, calls=%fused_computation.1.clone.1 | convolution fusion | flops 1082128384 | bytes 17833988 | tf_op jit(solution)/shard_map/while/body/eval_jaxpr/rgqd,kgd->rgqk/dot_general | solution.py:78
  280.8 8.6 %fusion.65 = f32[256,8]{0,1:T(8,128)S(1)} fusion(f32[2048,256,8]{1,0,2:T(8,128)} %get-tuple-element.217, f32[256,8]{0,1:T(8,128)S(1)} %bitcast.152), kind=kLoop, calls=%fused_computation.4.clone.1 | loop fusion | flops 12580864 | bytes 16793600 | tf_op jit(solution)/shard_map/while/body/eval_jaxpr/reduce_sum | solution.py:37
  289.5 7.6 %fusion.66 = f32[256,1,8,128]{0,3,2,1:T(8,128)S(1)} fusion(f32[2048,256,8]{1,0,2:T(8,128)} %get-tuple-element.217, f32[256,8]{0,1:T(8,128)S(1)} %bitcast.153, f32[256,1,8,128]{0,3,2,1:T(8,128)S(1)} %copy-done.1, bf16[2,16384,1,128]{3,1,2,0:T(8,128)(2,1)} %get-tuple-element.245, s32[]{:T(128)S(6)} %add.128, s32[]{:T(128)S(6)} %select_n.23, ...), kind=kOutput, calls=%fused_computation.8.clone.1 | convolution fusion | flops 1087111168 | bytes 19415048 | tf_op jit(solution)/shard_map/while/body/eval_jaxpr/rgqk,kgd->rgqd/dot_general | solution.py:38
  297.2 0.9 copy-done.2
  298.1 9.1 %bitcast_reduce_fusion.2 = (f32[256,8]{0,1:T(8,128)S(1)}, f32[2048,256,8]{1,0,2:T(8,128)}) fusion(bf16[256,1,8,128]{3,0,2,1:T(8,128)(2,1)S(1)} %get-tuple-element.246, bf16[2,16384,1,128]{3,1,2,0:T(8,128)(2,1)} %get-tuple-element.245, s32[]{:T(128)S(6)} %select_n.23), kind=kOutput, calls=%fused_computation.1.clone.1 | convolution fusion | flops 1082128384 | bytes 17833988 | tf_op jit(solution)/shard_map/while/body/eval_jaxpr/rgqd,kgd->rgqk/dot_general | solution.py:78
  307.2 8.6 %fusion.65 = f32[256,8]{0,1:T(8,128)S(1)} fusion(f32[2048,256,8]{1,0,2:T(8,128)} %get-tuple-element.217, f32[256,8]{0,1:T(8,128)S(1)} %bitcast.152), kind=kLoop, calls=%fused_computation.4.clone.1 | loop fusion | flops 12580864 | bytes 16793600 | tf_op jit(solution)/shard_map/while/body/eval_jaxpr/reduce_sum | solution.py:37
  315.8 7.6 %fusion.66 = f32[256,1,8,128]{0,3,2,1:T(8,128)S(1)} fusion(f32[2048,256,8]{1,0,2:T(8,128)} %get-tuple-element.217, f32[256,8]{0,1:T(8,128)S(1)} %bitcast.153, f32[256,1,8,128]{0,3,2,1:T(8,128)S(1)} %copy-done.1, bf16[2,16384,1,128]{3,1,2,0:T(8,128)(2,1)} %get-tuple-element.245, s32[]{:T(128)S(6)} %add.128, s32[]{:T(128)S(6)} %select_n.23, ...), kind=kOutput, calls=%fused_computation.8.clone.1 | convolution fusion | flops 1087111168 | bytes 19415048 | tf_op jit(solution)/shard_map/while/body/eval_jaxpr/rgqk,kgd->rgqd/dot_general | solution.py:38
  323.5 0.9 copy-done.2
  324.5 9.1 %bitcast_reduce_fusion.2 = (f32[256,8]{0,1:T(8,128)S(1)}, f32[2048,256,8]{1,0,2:T(8,128)}) fusion(bf16[256,1,8,128]{3,0,2,1:T(8,128)(2,1)S(1)} %get-tuple-element.246, bf16[2,16384,1,128]{3,1,2,0:T(8,128)(2,1)} %get-tuple-element.245, s32[]{:T(128)S(6)} %select_n.23), kind=kOutput, calls=%fused_computation.1.clone.1 | convolution fusion | flops 1082128384 | bytes 17833988 | tf_op jit(solution)/shard_map/while/body/eval_jaxpr/rgqd,kgd->rgqk/dot_general | solution.py:78
  333.6 8.6 %fusion.65 = f32[256,8]{0,1:T(8,128)S(1)} fusion(f32[2048,256,8]{1,0,2:T(8,128)} %get-tuple-element.217, f32[256,8]{0,1:T(8,128)S(1)} %bitcast.152), kind=kLoop, calls=%fused_computation.4.clone.1 | loop fusion | flops 12580864 | bytes 16793600 | tf_op jit(solution)/shard_map/while/body/eval_jaxpr/reduce_sum | solution.py:37
  342.2 7.6 %fusion.66 = f32[256,1,8,128]{0,3,2,1:T(8,128)S(1)} fusion(f32[2048,256,8]{1,0,2:T(8,128)} %get-tuple-element.217, f32[256,8]{0,1:T(8,128)S(1)} %bitcast.153, f32[256,1,8,128]{0,3,2,1:T(8,128)S(1)} %copy-done.1, bf16[2,16384,1,128]{3,1,2,0:T(8,128)(2,1)} %get-tuple-element.245, s32[]{:T(128)S(6)} %add.128, s32[]{:T(128)S(6)} %select_n.23, ...), kind=kOutput, calls=%fused_computation.8.clone.1 | convolution fusion | flops 1087111168 | bytes 19415048 | tf_op jit(solution)/shard_map/while/body/eval_jaxpr/rgqk,kgd->rgqd/dot_general | solution.py:38
  349.9 0.9 copy-done.2
  350.8 9.1 %bitcast_reduce_fusion.2 = (f32[256,8]{0,1:T(8,128)S(1)}, f32[2048,256,8]{1,0,2:T(8,128)}) fusion(bf16[256,1,8,128]{3,0,2,1:T(8,128)(2,1)S(1)} %get-tuple-element.246, bf16[2,16384,1,128]{3,1,2,0:T(8,128)(2,1)} %get-tuple-element.245, s32[]{:T(128)S(6)} %select_n.23), kind=kOutput, calls=%fused_computation.1.clone.1 | convolution fusion | flops 1082128384 | bytes 17833988 | tf_op jit(solution)/shard_map/while/body/eval_jaxpr/rgqd,kgd->rgqk/dot_general | solution.py:78
  359.9 8.6 %fusion.65 = f32[256,8]{0,1:T(8,128)S(1)} fusion(f32[2048,256,8]{1,0,2:T(8,128)} %get-tuple-element.217, f32[256,8]{0,1:T(8,128)S(1)} %bitcast.152), kind=kLoop, calls=%fused_computation.4.clone.1 | loop fusion | flops 12580864 | bytes 16793600 | tf_op jit(solution)/shard_map/while/body/eval_jaxpr/reduce_sum | solution.py:37
  368.5 7.6 %fusion.66 = f32[256,1,8,128]{0,3,2,1:T(8,128)S(1)} fusion(f32[2048,256,8]{1,0,2:T(8,128)} %get-tuple-element.217, f32[256,8]{0,1:T(8,128)S(1)} %bitcast.153, f32[256,1,8,128]{0,3,2,1:T(8,128)S(1)} %copy-done.1, bf16[2,16384,1,128]{3,1,2,0:T(8,128)(2,1)} %get-tuple-element.245, s32[]{:T(128)S(6)} %add.128, s32[]{:T(128)S(6)} %select_n.23, ...), kind=kOutput, calls=%fused_computation.8.clone.1 | convolution fusion | flops 1087111168 | bytes 19415048 | tf_op jit(solution)/shard_map/while/body/eval_jaxpr/rgqk,kgd->rgqd/dot_general | solution.py:38
  376.2 0.9 copy-done.2
  377.2 9.1 %bitcast_reduce_fusion.2 = (f32[256,8]{0,1:T(8,128)S(1)}, f32[2048,256,8]{1,0,2:T(8,128)}) fusion(bf16[256,1,8,128]{3,0,2,1:T(8,128)(2,1)S(1)} %get-tuple-element.246, bf16[2,16384,1,128]{3,1,2,0:T(8,128)(2,1)} %get-tuple-element.245, s32[]{:T(128)S(6)} %select_n.23), kind=kOutput, calls=%fused_computation.1.clone.1 | convolution fusion | flops 1082128384 | bytes 17833988 | tf_op jit(solution)/shard_map/while/body/eval_jaxpr/rgqd,kgd->rgqk/dot_general | solution.py:78
  386.3 8.6 %fusion.65 = f32[256,8]{0,1:T(8,128)S(1)} fusion(f32[2048,256,8]{1,0,2:T(8,128)} %get-tuple-element.217, f32[256,8]{0,1:T(8,128)S(1)} %bitcast.152), kind=kLoop, calls=%fused_computation.4.clone.1 | loop fusion | flops 12580864 | bytes 16793600 | tf_op jit(solution)/shard_map/while/body/eval_jaxpr/reduce_sum | solution.py:37
  394.9 7.6 %fusion.66 = f32[256,1,8,128]{0,3,2,1:T(8,128)S(1)} fusion(f32[2048,256,8]{1,0,2:T(8,128)} %get-tuple-element.217, f32[256,8]{0,1:T(8,128)S(1)} %bitcast.153, f32[256,1,8,128]{0,3,2,1:T(8,128)S(1)} %copy-done.1, bf16[2,16384,1,128]{3,1,2,0:T(8,128)(2,1)} %get-tuple-element.245, s32[]{:T(128)S(6)} %add.128, s32[]{:T(128)S(6)} %select_n.23, ...), kind=kOutput, calls=%fused_computation.8.clone.1 | convolution fusion | flops 1087111168 | bytes 19415048 | tf_op jit(solution)/shard_map/while/body/eval_jaxpr/rgqk,kgd->rgqd/dot_general | solution.py:38
  402.6 0.9 copy-done.2
  403.5 1.9 fusion.21
  405.5 4.9 %fusion.26 = bf16[256,1,8,128]{0,3,2,1:T(8,128)(2,1)S(1)} fusion(f32[256,1,8,256]{0,3,2,1:T(8,128)} %get-tuple-element.173, f32[256,8]{0,1:T(8,128)S(1)} %fusion.47, f32[256,1,8,128]{0,3,2,1:T(8,128)} %get-tuple-element.116, bf16[8192,128]{1,0:T(8,128)(2,1)S(1)} %copy-done, f32[256,8]{0,1:T(8,128)S(1)} %get-tuple-element.169, ...), kind=kOutput, calls=%fused_computation.36 | convolution fusion | flops 681869312 | bytes 10020096 | tf_op jit(solution)/shard_map/rgqk,kgd->rgqd/dot_general | solution.py:38
  410.4 1.0 copy.34
  (71 shorter events, 1.8 us)
Async XLA Ops:
  6.5 398.9 %copy-start = (bf16[8192,128]{1,0:T(8,128)(2,1)S(1)}, bf16[8192,128]{1,0:T(8,128)(2,1)}, u32[]{:S(2)}) copy-start(bf16[8192,128]{1,0:T(8,128)(2,1)} %param.13) | copy-start | bytes 6291460
  6.5 78.6 %all-gather.2.cloned.1.call-start = ((), (), s32[]{:S(2)}) async-start(), calls=%async_computation.1 | async-start | bytes 8912896 | tf_op jit(solution)/shard_map/all_gather | solution.py:88
  8.7 85.3 %copy-start.5 = (f32[8192]{0:T(1024)S(1)}, f32[8192]{0:T(1024)}, u32[]{:S(2)}) copy-start(f32[8192]{0:T(1024)} %param.10) | copy-start | bytes 98308
  85.2 100.1 %all-to-all-start = ((bf16[2,2048,8,128]{3,1,0,2:T(8,128)(2,1)}), bf16[2,2048,8,128]{3,1,0,2:T(8,128)(2,1)}, u32[]{:S(2)}, u32[]{:S(2)}) async-start(bf16[2,2048,8,128]{3,1,0,2:T(8,128)(2,1)} %all-gather.2.cloned.1.call-done), calls=%async_computation | async-start | bytes 16777216 | tf_op jit(solution)/shard_map/all_to_all | solution.py:89
  103.5 2.2 copy-start.3
  103.5 2.9 copy-start.4
  201.8 8.6 %copy-start.1 = (f32[256,1,8,128]{0,3,2,1:T(8,128)S(1)}, f32[256,1,8,128]{0,3,2,1:T(8,128)}, u32[]{:S(2)}) copy-start(f32[256,1,8,128]{0,3,2,1:T(8,128)} %get-tuple-element.233) | copy-start | bytes 3145732 | tf_op jit(solution)/shard_map/while
  218.1 1.0 copy-start.2
  228.1 8.6 %copy-start.1 = (f32[256,1,8,128]{0,3,2,1:T(8,128)S(1)}, f32[256,1,8,128]{0,3,2,1:T(8,128)}, u32[]{:S(2)}) copy-start(f32[256,1,8,128]{0,3,2,1:T(8,128)} %get-tuple-element.233) | copy-start | bytes 3145732 | tf_op jit(solution)/shard_map/while
  244.4 1.0 copy-start.2
  254.5 8.6 %copy-start.1 = (f32[256,1,8,128]{0,3,2,1:T(8,128)S(1)}, f32[256,1,8,128]{0,3,2,1:T(8,128)}, u32[]{:S(2)}) copy-start(f32[256,1,8,128]{0,3,2,1:T(8,128)} %get-tuple-element.233) | copy-start | bytes 3145732 | tf_op jit(solution)/shard_map/while
  270.8 1.0 copy-start.2
  280.8 8.6 %copy-start.1 = (f32[256,1,8,128]{0,3,2,1:T(8,128)S(1)}, f32[256,1,8,128]{0,3,2,1:T(8,128)}, u32[]{:S(2)}) copy-start(f32[256,1,8,128]{0,3,2,1:T(8,128)} %get-tuple-element.233) | copy-start | bytes 3145732 | tf_op jit(solution)/shard_map/while
  297.1 1.0 copy-start.2
  307.2 8.6 %copy-start.1 = (f32[256,1,8,128]{0,3,2,1:T(8,128)S(1)}, f32[256,1,8,128]{0,3,2,1:T(8,128)}, u32[]{:S(2)}) copy-start(f32[256,1,8,128]{0,3,2,1:T(8,128)} %get-tuple-element.233) | copy-start | bytes 3145732 | tf_op jit(solution)/shard_map/while
  323.5 1.0 copy-start.2
  333.6 8.6 %copy-start.1 = (f32[256,1,8,128]{0,3,2,1:T(8,128)S(1)}, f32[256,1,8,128]{0,3,2,1:T(8,128)}, u32[]{:S(2)}) copy-start(f32[256,1,8,128]{0,3,2,1:T(8,128)} %get-tuple-element.233) | copy-start | bytes 3145732 | tf_op jit(solution)/shard_map/while
  349.8 1.0 copy-start.2
  359.9 8.6 %copy-start.1 = (f32[256,1,8,128]{0,3,2,1:T(8,128)S(1)}, f32[256,1,8,128]{0,3,2,1:T(8,128)}, u32[]{:S(2)}) copy-start(f32[256,1,8,128]{0,3,2,1:T(8,128)} %get-tuple-element.233) | copy-start | bytes 3145732 | tf_op jit(solution)/shard_map/while
  376.2 1.0 copy-start.2
  386.3 8.6 %copy-start.1 = (f32[256,1,8,128]{0,3,2,1:T(8,128)S(1)}, f32[256,1,8,128]{0,3,2,1:T(8,128)}, u32[]{:S(2)}) copy-start(f32[256,1,8,128]{0,3,2,1:T(8,128)} %get-tuple-element.233) | copy-start | bytes 3145732 | tf_op jit(solution)/shard_map/while
  402.6 1.0 copy-start.2
Sparse Core Ops, SparseCore 0:
  9.8 75.3 all-gather.1
where the time goes:
time: 419 us; the launch traced here: 418 us
  matrix products  152 us (36%)
  waiting for transfers between devices  151 us (36%)
  other arithmetic  75.7 us (18%)
  local copies, waits for them, and re-layouts  19.6 us (5%)
  between operations  14.2 us (3%)
  starting transfers between devices  4.95 us (1%)
    all_gather x1, waiting for transfers between devices, shards(): gathered = lax.all_gather(prompt_cache, 'rollout', axis=1, tiled=True)  76.5 us
    all_to_all x1, waiting for transfers between devices, shards(): lax.all_to_all(gathered, 'tp', split_axis=2, concat_axis=1, tiled=True)  74.8 us
    dot_general x8, matrix products, absorb(): jnp.einsum('rgqd,kgd->rgqk', query_matrix, piece[0], preferred_element_ty...  72.7 us
    reduce_sum x9, other arithmetic, update(): row_sum = row_sum * factor + weights.sum(axis=-1)  70.8 us
    dot_general x9, matrix products, update(): jnp.einsum('rgqk,kgd->rgqd', weights.astype(jnp.bfloat16), values, prefer...  66.1 us
    dot_general x1, matrix products, shards(): jnp.dot(normalized_input, query_weight, preferred_element_type=jnp.float32)  9.55 us
  transfers between devices with their start and end apart: 2, of which 2 were waited for; matrix products, arithmetic and copies ran while one was open for 4% of the time, Pallas kernels for 0%

commit v1 on v0

v1 whole, which is shorter than its diff:
```python
import functools

import jax
import jax.numpy as jnp
import numpy as np
from jax import lax
from jax.experimental import pallas as pl
from jax.experimental.pallas import tpu as pltpu
from jax.sharding import PartitionSpec as P

F32, BF16 = jnp.float32, jnp.bfloat16
MESH = pl.DeviceIdType.MESH
HEAD = 128
ROWS = 256
GROUP = 8
WIDTH = 8192
PARTS = 8
PART = WIDTH // PARTS
TP, ROLLOUT = 8, 16
PIECE = 128
CHUNK = PIECE * TP
PROMPT = CHUNK * ROLLOUT
ROPE_BASE = 500000.0
SCALE = float(HEAD ** -0.5 * np.log2(np.e))

OWN, SIB_OWN, UP, DOWN, SIB_UP, SIB_DOWN, ACROSS, SIB_ACROSS = range(8)
FAR, SIB_FAR, UP_A, DOWN_A, SIB_UP_A, SIB_DOWN_A, FAR_A, SIB_FAR_A = range(8, 16)


def tables():
    half = HEAD // 2
    frequency = np.power(
        np.float32(ROPE_BASE), -2.0 * np.arange(half, dtype=np.float32) / np.float32(HEAD)
    ).astype(np.float32)
    position = (PROMPT + np.arange(ROWS)).astype(np.float32)
    angles = (position[:, None] * frequency[None, :]).astype(np.float32).astype(np.float64)
    cosine, sine = np.cos(angles), np.sin(angles)
    return (
        np.concatenate([cosine, cosine], axis=1).astype(np.float32),
        np.concatenate([-sine, sine], axis=1).astype(np.float32),
    )


def kernel(
    tokens, gain, wq, wk, wv, cache, length, cos_ref, sin_ref, out,
    tok, normed, wq_v, wk_v, wv_v, proj, kv, q, fresh, top, acc,
    tok_sem, w_sem, own_sem, a_send, a_recv, send, recv,
):
    r, t = lax.axis_index("rollout"), lax.axis_index("tp")
    y, low = r // 4, r % 4
    core, across = r % 2, (r // 2) % 2
    sibling = r + 1 - 2 * core
    partner = r + 2 - 4 * across
    up = ((y + 1) % 4) * 4 + low
    down = ((y + 3) % 4) * 4 + low
    half = CHUNK // 2

    def tok_copy(i):
        return pltpu.make_async_copy(
            tokens.at[:, pl.ds(pl.multiple_of(i * PART, PART), PART)], tok.at[i], tok_sem.at[i]
        )

    def w_copies(i):
        rows = pl.ds(pl.multiple_of(i * PART, PART), PART)
        return [
            pltpu.make_async_copy(wq.at[rows], wq_v.at[i], w_sem.at[0, i]),
            pltpu.make_async_copy(wk.at[rows], wk_v.at[i], w_sem.at[1, i]),
            pltpu.make_async_copy(wv.at[rows], wv_v.at[i], w_sem.at[2, i]),
        ]

    def start_loads(i, _):
        tok_copy(i).start()
        return 0

    def start_weights(i, _):
        for c in w_copies(i):
            c.start()
        return 0

    lax.fori_loop(0, PARTS, start_loads, 0)
    lax.fori_loop(0, PARTS, start_weights, 0)

    barrier = pltpu.get_barrier_semaphore()
    for d in range(1, TP):
        pl.semaphore_signal(barrier, inc=1, device_id=(r, (t + d) % TP), device_id_type=MESH)
    for other in (sibling, partner, up, down):
        pl.semaphore_signal(barrier, inc=1, device_id=(other, t), device_id_type=MESH)
    pl.semaphore_wait(barrier, TP - 1 + 4)

    def a_copy(d):
        head = (t + d) % TP
        return pltpu.make_async_remote_copy(
            src_ref=cache.at[head],
            dst_ref=kv.at[OWN, :, pl.ds(pl.multiple_of(t * PIECE, PIECE), PIECE)],
            send_sem=a_send.at[d - 1], recv_sem=a_recv.at[d - 1],
            device_id=(r, head), device_id_type=MESH,
        )

    def a_arrival(d):
        source = (t + TP - d) % TP
        return pltpu.make_async_remote_copy(
            src_ref=cache.at[t],
            dst_ref=kv.at[OWN, :, pl.ds(pl.multiple_of(source * PIECE, PIECE), PIECE)],
            send_sem=a_send.at[d - 1], recv_sem=a_recv.at[d - 1],
            device_id=(r, t), device_id_type=MESH,
        )

    own = pltpu.make_async_copy(
        cache.at[t], kv.at[OWN, :, pl.ds(pl.multiple_of(t * PIECE, PIECE), PIECE)], own_sem
    )
    for d in range(1, TP):
        a_copy(d).start()
    own.start()

    moves = {}

    def move(name, source, target, device, rows=None):
        index = len(moves)
        if rows is None:
            src, dst = kv.at[source], kv.at[target]
        else:
            src, dst = kv.at[source, :, rows], kv.at[target, :, rows]
        moves[name] = pltpu.make_async_remote_copy(
            src_ref=src, dst_ref=dst, send_sem=send.at[index], recv_sem=recv.at[index],
            device_id=(device, t), device_id_type=MESH,
        )

    first, second = pl.ds(0, half), pl.ds(half, half)
    move("own_across", OWN, ACROSS, partner)
    move("own_up", OWN, UP, up)
    move("own_down", OWN, DOWN, down)
    move("sib_own", OWN, SIB_OWN, sibling)
    move("sib_up", UP, SIB_UP, sibling)
    move("sib_down", DOWN, SIB_DOWN, sibling)
    move("far_up", UP, FAR, up, first)
    move("far_down", DOWN, FAR, down, second)
    move("sib_across", ACROSS, SIB_ACROSS, sibling)
    move("across_up", ACROSS, UP_A, up)
    move("across_down", ACROSS, DOWN_A, down)
    move("sib_far", FAR, SIB_FAR, sibling)
    move("sib_up_a", UP_A, SIB_UP_A, sibling)
    move("sib_down_a", DOWN_A, SIB_DOWN_A, sibling)
    move("far_up_a", UP_A, FAR_A, up, first)
    move("far_down_a", DOWN_A, FAR_A, down, second)
    move("sib_far_a", FAR_A, SIB_FAR_A, sibling)

    def square(i, total):
        tok_copy(i).wait()
        x = tok[i].astype(F32)
        x = x * x
        return total + sum(x[:, j * 128:(j + 1) * 128] for j in range(PART // 128))

    total = lax.fori_loop(0, PARTS, square, jnp.zeros((ROWS, 128), F32))
    factor = lax.rsqrt(jnp.sum(total, axis=1, keepdims=True) * (1.0 / WIDTH) + 1e-5)

    def scale(i, _):
        normed[i] = (tok[i].astype(F32) * factor * gain[i]).astype(BF16)
        return 0

    lax.fori_loop(0, PARTS, scale, 0)

    def project(i, _):
        for c in w_copies(i):
            c.wait()
        x = normed[i]
        pieces = [
            jnp.dot(x, wq_v[i], preferred_element_type=F32),
            jnp.dot(x, wk_v[i], preferred_element_type=F32),
            jnp.dot(x, wv_v[i], preferred_element_type=F32),
        ]
        spans = [(0, 1024), (1024, 1152), (1152, 1280)]

        @pl.when(i == 0)
        def _():
            for (a, b), piece in zip(spans, pieces):
                proj[:, a:b] = piece

        @pl.when(i > 0)
        def _():
            for (a, b), piece in zip(spans, pieces):
                proj[:, a:b] += piece

        @pl.when(i == 4)
        def _():
            for d in range(1, TP):
                a_arrival(d).wait_recv()
            own.wait()
            for name in ("own_across", "own_up", "own_down", "sib_own"):
                moves[name].start()

        return 0

    lax.fori_loop(0, PARTS, project, 0)

    def rotate(u):
        return u * cos_ref[...] + pltpu.roll(u, HEAD // 2, 1) * sin_ref[...]

    for h in range(GROUP):
        u = rotate(proj[:, h * HEAD:(h + 1) * HEAD])
        q[h * ROWS:(h + 1) * ROWS, :] = (u * SCALE).astype(BF16)
    fresh[0] = rotate(proj[:, 1024:1152]).astype(BF16)
    fresh[1] = proj[:, 1152:1280].astype(BF16)

    def attend(h, keys, values, near=None):
        rows = pl.ds(h * ROWS, ROWS)
        scores = lax.dot_general(
            q[rows, :], keys, (((1,), (1,)), ((), ())), preferred_element_type=F32
        )
        if near is not None:
            scores = jnp.where(near, scores, -1e30)
        peak = jnp.max(scores, axis=1, keepdims=True)
        if near is None:
            before = top[rows, :]
            peak = jnp.maximum(before, peak)
            fade = jnp.exp2(before - peak)
            top[rows, :] = peak
            level = peak[:, 0:1]
        else:
            top[rows, :] = jnp.broadcast_to(peak, (ROWS, 128))
            level = peak
        weights = jnp.exp2(scores - level).astype(BF16)
        wide = jnp.concatenate([values, jnp.ones_like(values)], axis=1)
        part = jnp.dot(weights, wide, preferred_element_type=F32)
        if near is None:
            acc[rows, :] = acc[rows, :] * jnp.concatenate([fade, fade], axis=1) + part
        else:
            acc[rows, :] = part

    causal = (
        lax.broadcasted_iota(jnp.int32, (ROWS, ROWS), 1)
        <= lax.broadcasted_iota(jnp.int32, (ROWS, ROWS), 0)
    )
    for h in range(GROUP):
        attend(h, fresh[0], fresh[1], causal)

    def step(i, _):
        @pl.when(i == 0)
        def _():
            moves["sib_own"].wait_recv()

        @pl.when(i == 1)
        def _():
            moves["own_up"].wait_recv()
            moves["own_down"].wait_recv()
            for name in ("far_up", "far_down", "sib_up", "sib_down"):
                moves[name].start()

        @pl.when(i == 2)
        def _():
            moves["own_across"].wait_recv()
            for name in ("across_up", "across_down", "sib_across"):
                moves[name].start()
            moves["sib_up"].wait_recv()
            moves["sib_down"].wait_recv()

        @pl.when(i == 3)
        def _():
            moves["sib_across"].wait_recv()
            moves["far_up"].wait_recv()
            moves["far_down"].wait_recv()
            moves["sib_far"].start()

        @pl.when(i == 4)
        def _():
            moves["sib_far"].wait_recv()

        @pl.when(i == 5)
        def _():
            moves["across_up"].wait_recv()
            moves["across_down"].wait_recv()
            for name in ("far_up_a", "far_down_a", "sib_up_a", "sib_down_a"):
                moves[name].start()

        @pl.when(i == 6)
        def _():
            moves["sib_up_a"].wait_recv()
            moves["sib_down_a"].wait_recv()
            moves["far_up_a"].wait_recv()
            moves["far_down_a"].wait_recv()
            moves["sib_far_a"].start()

        @pl.when(i == 7)
        def _():
            moves["sib_far_a"].wait_recv()

        for j in range(2):
            for h in range(GROUP):
                attend(h, kv[2 * i + j, 0], kv[2 * i + j, 1])
        return 0

    lax.fori_loop(0, ROLLOUT // 2, step, 0)

    live = lax.broadcasted_iota(jnp.int32, (ROWS, HEAD), 0) < length[0]
    for h in range(GROUP):
        rows = pl.ds(h * ROWS, ROWS)
        result = acc[rows, 0:HEAD] / acc[rows, HEAD:2 * HEAD]
        out[:, h * HEAD:(h + 1) * HEAD] = jnp.where(live, result, 0.0).astype(BF16)

    for d in range(1, TP):
        a_copy(d).wait_send()
    for copy in moves.values():
        copy.wait_send()


def shards(tokens, norm_gain, query_weight, key_matrix, value_matrix, prompt_cache, lengths):
    by_head = jnp.transpose(prompt_cache, (2, 0, 1, 3))
    gain = norm_gain.reshape(PARTS, 1, PART)
    cosine, sine = tables()
    hbm = pl.BlockSpec(memory_space=pl.ANY)
    vmem = pl.BlockSpec(memory_space=pltpu.VMEM)
    smem = pl.BlockSpec(memory_space=pltpu.SMEM)
    return pl.pallas_call(
        kernel,
        out_shape=jax.ShapeDtypeStruct((ROWS, GROUP * HEAD), BF16),
        in_specs=[hbm, vmem, hbm, hbm, hbm, hbm, smem, vmem, vmem],
        out_specs=vmem,
        scratch_shapes=[
            pltpu.VMEM((PARTS, ROWS, PART), BF16),
            pltpu.VMEM((PARTS, ROWS, PART), BF16),
            pltpu.VMEM((PARTS, PART, GROUP * HEAD), BF16),
            pltpu.VMEM((PARTS, PART, HEAD), BF16),
            pltpu.VMEM((PARTS, PART, HEAD), BF16),
            pltpu.VMEM((ROWS, (GROUP + 2) * HEAD), F32),
            pltpu.VMEM((ROLLOUT, 2, CHUNK, HEAD), BF16),
            pltpu.VMEM((GROUP * ROWS, HEAD), BF16),
            pltpu.VMEM((2, ROWS, HEAD), BF16),
            pltpu.VMEM((GROUP * ROWS, 128), F32),
            pltpu.VMEM((GROUP * ROWS, 2 * HEAD), F32),
            pltpu.SemaphoreType.DMA((PARTS,)),
            pltpu.SemaphoreType.DMA((3, PARTS)),
            pltpu.SemaphoreType.DMA,
            pltpu.SemaphoreType.DMA((TP - 1,)),
            pltpu.SemaphoreType.DMA((TP - 1,)),
            pltpu.SemaphoreType.DMA((17,)),
            pltpu.SemaphoreType.DMA((17,)),
        ],
        compiler_params=pltpu.CompilerParams(
            collective_id=0, has_side_effects=True, vmem_limit_bytes=62 << 20
        ),
        cost_estimate=pl.CostEstimate(
            flops=23_000_000_000, bytes_accessed=30_000_000, transcendentals=34_000_000
        ),
    )(
        tokens, gain, query_weight, key_matrix, value_matrix, by_head, lengths,
        jnp.asarray(cosine), jnp.asarray(sine),
    )


def solution(mesh):
    placed = (
        P("rollout", None),
        P(),
        P(None, "tp"),
        P(None, "tp"),
        P(None, "tp"),
        P(None, ("rollout", "tp"), None, None),
        P("rollout"),
    )
    return jax.shard_map(
        shards, mesh=mesh, in_specs=placed, out_specs=P("rollout", "tp"), check_vma=False
    )
```

time: 419 us -> 76.4 us (0.18)
  matrix products: 152 us -> 0 us
  waiting for transfers between devices: 151 us -> 0 us
  other arithmetic: 75.7 us -> 0 us
  Pallas kernels: 0 us -> 71.7 us
  local copies, waits for them, and re-layouts: 19.6 us -> 3.81 us
  between operations: 14.2 us -> 0.66 us
  starting transfers between devices: 4.95 us -> 0 us
    dot_general x20 -> x0, matrix products: 152 us -> none  [the longest x8 72.7 us: absorb(): jnp.einsum('rgqd,kgd->rgqk', query_matrix, piece[0], preferred_element_ty...]
    all_gather x1 -> x0, waiting for transfers between devices: 76.5 us -> none  [shards(): gathered = lax.all_gather(prompt_cache, 'rollout', axis=1, tiled=True)]
    all_to_all x1 -> x0, waiting for transfers between devices: 74.8 us -> none  [shards(): lax.all_to_all(gathered, 'tp', split_axis=2, concat_axis=1, tiled=True)]
    reduce_sum x10 -> x0, other arithmetic: 73.9 us -> none  [the longest x9 70.8 us: update(): row_sum = row_sum * factor + weights.sum(axis=-1)]
    pallas_call x0 -> x1, Pallas kernels: none -> 71.7 us  [shards(): pl.pallas_call(kernel, out_shape=jax.ShapeDtypeStruct((ROWS, GROUP * HEAD...]
    while x40 -> x0, local copies, waits for them, and re-layouts: 7.54 us -> none
    all_to_all x1 -> x0, local copies, waits for them, and re-layouts: 7.42 us -> none  [shards(): lax.all_to_all(gathered, 'tp', split_axis=2, concat_axis=1, tiled=True)]
    all_to_all x1 -> x0, starting transfers between devices: 4.95 us -> none  [shards(): lax.all_to_all(gathered, 'tp', split_axis=2, concat_axis=1, tiled=True)]
  transfers between devices with their start and end apart: 2 -> 0, of which waited for: 2 -> 0; matrix products, arithmetic and copies ran while one was open for 4% -> 0% of each run, Pallas kernels for 0% -> 0%
where the time goes in v1:
time: 76.4 us; the launch traced here: 76.1 us
  Pallas kernels  71.7 us (94%)
  local copies, waits for them, and re-layouts  3.81 us (5%)
    pallas_call x1, Pallas kernels, shards(): pl.pallas_call(kernel, out_shape=jax.ShapeDtypeStruct((ROWS, GROUP * HEAD...  71.7 us
    unnamed x2, local copies, waits for them, and re-layouts  3.81 us

profile of v1, /device:TPU:0, one launch (start us, length us, event | category | flops | bytes accessed | tf_op | source)
XLA Modules:
  0.0 76.1 jit_solution(15790464581461292899)
XLA Ops:
  0.7 1.9 %copy.12 = bf16[2,128,8,128]{3,1,0,2:T(8,128)(2,1)} copy(bf16[2,128,8,128]{3,2,1,0:T(8,128)(2,1)} %param.14) | data formatting | bytes 1048576 | tf_op args[5]
  2.6 71.7 %shard_map.91 = bf16[256,1024]{1,0:T(8,128)(2,1)} custom-call(bf16[256,8192]{1,0:T(8,128)(2,1)} %tokens.1, f32[8,1,1024]{2,1,0:T(1,128)} %bitcast.5, bf16[8192,1024]{1,0:T(8,128)(2,1)} %wq.1, bf16[8192,128]{1,0:T(8,128)(2,1)} %wk.1, bf16[8192,128]{1,0:T(8,128)(2,1)} %wv.1, bf16[8,2,128,128]{3,2,1,0:T(8,128)(2,1)} %bitcast.4, s32[1]{0:T(128)S(6)} %copy.14.length, ...), custom_call_target="tpu_custom_call" | custom-call | flops 23000000512 | bytes 30000000 | tf_op jit(solution)/shard_map/pallas_call | solution.py:312
  74.3 1.9 %copy.15 = bf16[256,1024]{1,0:T(8,128)(2,1)} copy(bf16[256,1024]{1,0:T(8,128)(2,1)} %shard_map.91) | data formatting | bytes 1048576

commit v2 on v1

v2 whole, which is shorter than its diff:
```python
import functools

import jax
import jax.numpy as jnp
import numpy as np
from jax import lax
from jax.experimental import pallas as pl
from jax.experimental.pallas import tpu as pltpu
from jax.sharding import PartitionSpec as P

F32, BF16 = jnp.float32, jnp.bfloat16
MESH = pl.DeviceIdType.MESH
HEAD = 128
ROWS = 256
GROUP = 8
WIDTH = 8192
PARTS = 8
PART = WIDTH // PARTS
TP, ROLLOUT = 8, 16
PIECE = 128
CHUNK = PIECE * TP
PROMPT = CHUNK * ROLLOUT
ROPE_BASE = 500000.0
SCALE = float(HEAD ** -0.5 * np.log2(np.e))

HALF = CHUNK // 2
EARLY = 4
TILE = 2048
SPAN = 256
OFFSETS = ((0, 0), (0, 1), (1, 0), (3, 0), (1, 1), (3, 1), (2, 0), (2, 1))
OWN, NEAR_A, ACROSS, NEAR_B, ACROSS_A, FAR, ACROSS_B, FAR_ACROSS = range(8)
SLOT = {NEAR_A: 1, ACROSS: 3, NEAR_B: 4, ACROSS_A: 7, FAR: 9, ACROSS_B: 10, FAR_ACROSS: 13}
SIBLING_SLOT = (0, 2, 5, 6, 8, 11, 12, 14)


def tables():
    half = HEAD // 2
    frequency = np.power(
        np.float32(ROPE_BASE), -2.0 * np.arange(half, dtype=np.float32) / np.float32(HEAD)
    ).astype(np.float32)
    position = (PROMPT + np.arange(ROWS)).astype(np.float32)
    angles = (position[:, None] * frequency[None, :]).astype(np.float32).astype(np.float64)
    cosine, sine = np.cos(angles), np.sin(angles)
    return (
        np.concatenate([cosine, cosine], axis=1).astype(np.float32),
        np.concatenate([-sine, sine], axis=1).astype(np.float32),
    )


def kernel(
    tokens, gain, wq, wk, wv, cache, length, cos_ref, sin_ref, out,
    tok, normed, wq_v, wk_v, wv_v, proj, raw, wide, by_head, home, kv, q, top, acc,
    tok_sem, w_sem, raw_sem, a_send, a_recv, send, recv,
):
    r, t = lax.axis_index("rollout"), lax.axis_index("tp")
    y, low = r // 4, r % 4
    core, across = r % 2, (r // 2) % 2
    sibling = r + 1 - 2 * core
    partner = r + 2 - 4 * across
    up = ((y + 1) % 4) * 4 + low
    down = ((y + 3) % 4) * 4 + low

    def tp_device(d):
        dz, dx = OFFSETS[d]
        z, x = t // 2, t % 2
        return ((z + dz) % 4) * 2 + (x + dx) % 2

    barrier = pltpu.get_barrier_semaphore()
    for d in range(1, TP):
        pl.semaphore_signal(barrier, inc=1, device_id=(r, tp_device(d)), device_id_type=MESH)
    for other in (sibling, partner, up, down):
        pl.semaphore_signal(barrier, inc=1, device_id=(other, t), device_id_type=MESH)

    raw_copy = pltpu.make_async_copy(cache, raw, raw_sem)
    raw_copy.start()

    def tok_copy(i):
        return pltpu.make_async_copy(
            tokens.at[:, pl.ds(pl.multiple_of(i * PART, PART), PART)], tok.at[i], tok_sem.at[i]
        )

    def w_copies(i):
        rows = pl.ds(pl.multiple_of(i * PART, PART), PART)
        return [
            pltpu.make_async_copy(wq.at[rows], wq_v.at[i], w_sem.at[0, i]),
            pltpu.make_async_copy(wk.at[rows], wk_v.at[i], w_sem.at[1, i]),
            pltpu.make_async_copy(wv.at[rows], wv_v.at[i], w_sem.at[2, i]),
        ]

    def start_loads(i, _):
        tok_copy(i).start()
        return 0

    def start_weights(i, _):
        for c in w_copies(i):
            c.start()
        return 0

    lax.fori_loop(0, PARTS, start_loads, 0)
    lax.fori_loop(0, EARLY, start_weights, 0)

    raw_copy.wait()
    wide[...] = raw[...].astype(F32)
    for g in range(TP):
        piece = wide[pl.ds(g, 2 * PIECE, stride=TP), :].astype(BF16)
        by_head[g, 0] = piece[:PIECE]
        by_head[g, 1] = piece[PIECE:]


    def a_copy(d):
        head = tp_device(d)
        return pltpu.make_async_remote_copy(
            src_ref=by_head.at[head],
            dst_ref=home.at[:, pl.ds(d * PIECE, PIECE)],
            send_sem=a_send.at[d - 1], recv_sem=a_recv.at[d - 1],
            device_id=(r, head), device_id_type=MESH,
        )


    first, second = pl.ds(0, HALF), pl.ds(HALF, HALF)
    quarters = [pl.ds(j * HALF // 2, HALF // 2) for j in range(4)]
    moves = {}

    def spot(block, rows):
        if block == 0:
            return home.at[:, rows]
        return kv.at[SLOT[block], :, rows]

    def move(name, source, source_rows, target, target_rows, device):
        index = len(moves)
        moves[name] = pltpu.make_async_remote_copy(
            src_ref=spot(source, source_rows), dst_ref=spot(target, target_rows),
            send_sem=send.at[index], recv_sem=recv.at[index],
            device_id=(device, t), device_id_type=MESH,
        )

    move("own_a_up", 0, first, NEAR_A, first, up)
    move("own_a_down", 0, first, NEAR_A, second, down)
    move("own_a_across", 0, first, ACROSS, first, partner)
    move("own_b_up", 0, second, NEAR_B, first, up)
    move("own_b_down", 0, second, NEAR_B, second, down)
    move("own_b_across", 0, second, ACROSS, second, partner)
    move("far_a", NEAR_A, first, FAR, first, up)
    move("far_b", NEAR_B, second, FAR, second, down)
    move("across_a_up", ACROSS, first, ACROSS_A, first, up)
    move("across_a_down", ACROSS, first, ACROSS_A, second, down)
    move("up_b_across", NEAR_B, first, ACROSS_B, first, partner)
    move("down_b_across", NEAR_B, second, ACROSS_B, second, partner)
    move("far_b_across", FAR, second, FAR_ACROSS, second, partner)
    move("far_across_up", ACROSS_A, quarters[0], FAR_ACROSS, quarters[0], up)
    move("far_across_down", ACROSS_A, quarters[3], FAR_ACROSS, quarters[1], down)
    whole = pl.ds(0, CHUNK)
    for block in range(8):
        index = len(moves)
        moves["sibling", block] = pltpu.make_async_remote_copy(
            src_ref=spot(block, whole), dst_ref=kv.at[SIBLING_SLOT[block]],
            send_sem=send.at[index], recv_sem=recv.at[index],
            device_id=(sibling, t), device_id_type=MESH,
        )

    def start(*names):
        for name in names:
            moves[name].start()

    def arrived(*names):
        for name in names:
            moves[name].wait_recv()

    def square(i, total):
        tok_copy(i).wait()
        x = tok[i].astype(F32)
        x = x * x
        return total + sum(x[:, j * 128:(j + 1) * 128] for j in range(PART // 128))

    total = lax.fori_loop(0, PARTS, square, jnp.zeros((ROWS, 128), F32))
    factor = lax.rsqrt(jnp.sum(total, axis=1, keepdims=True) * (1.0 / WIDTH) + 1e-5)

    def scale(i, _):
        normed[i] = (tok[i].astype(F32) * factor * gain[i]).astype(BF16)
        return 0

    lax.fori_loop(0, PARTS, scale, 0)

    pl.semaphore_wait(barrier, TP - 1 + 4)
    for d in range(1, TP):
        a_copy(d).start()
    lax.fori_loop(EARLY, PARTS, start_weights, 0)
    home[:, 0:PIECE, :] = by_head[t]

    def project(i, _):
        for c in w_copies(i):
            c.wait()
        x = normed[i]
        pieces = [
            jnp.dot(x, wq_v[i], preferred_element_type=F32),
            jnp.dot(x, wk_v[i], preferred_element_type=F32),
            jnp.dot(x, wv_v[i], preferred_element_type=F32),
        ]
        spans = [(0, 1024), (1024, 1152), (1152, 1280)]

        @pl.when(i == 0)
        def _():
            for (a, b), piece in zip(spans, pieces):
                proj[:, a:b] = piece

        @pl.when(i > 0)
        def _():
            for (a, b), piece in zip(spans, pieces):
                proj[:, a:b] += piece

        @pl.when(i == PARTS - 1)
        def _():
            for d in range(1, 4):
                a_copy(d).wait_recv()
            start("own_a_up", "own_a_down", "own_a_across")

        return 0

    lax.fori_loop(0, PARTS, project, 0)

    def rotate(u):
        return u * cos_ref[...] + pltpu.roll(u, HEAD // 2, 1) * sin_ref[...]

    for h in range(GROUP):
        u = rotate(proj[:, h * HEAD:(h + 1) * HEAD])
        q[h * ROWS:(h + 1) * ROWS, :] = (u * SCALE).astype(BF16)
    home[0, CHUNK:, :] = rotate(proj[:, 1024:1152]).astype(BF16)
    home[1, CHUNK:, :] = proj[:, 1152:1280].astype(BF16)

    for d in range(4, TP):
        a_copy(d).wait_recv()
    start("own_b_up", "own_b_down", "own_b_across", ("sibling", OWN))

    def attend(start, count, keys, values, near=None):
        rows = pl.ds(start, count)
        scores = lax.dot_general(
            q[rows, :], keys, (((1,), (1,)), ((), ())), preferred_element_type=F32
        )
        if near is not None:
            scores = jnp.where(near, scores, -1e30)
        peak = jnp.max(scores, axis=1, keepdims=True)
        if near is None:
            before = top[rows, :]
            peak = jnp.maximum(before, peak)
            fade = jnp.exp2(before - peak)
        else:
            peak = jnp.broadcast_to(peak, (count, 128))
        top[rows, :] = peak
        weights = jnp.concatenate(
            [jnp.exp2(scores[:, j:j + 128] - peak) for j in range(0, SPAN, 128)], axis=1
        ).astype(BF16)
        both = jnp.concatenate([values, jnp.ones_like(values)], axis=1)
        part = jnp.dot(weights, both, preferred_element_type=F32)
        if near is None:
            acc[rows, :] = acc[rows, :] * jnp.concatenate([fade, fade], axis=1) + part
        else:
            acc[rows, :] = part

    def absorb(block):
        for j in range(0, CHUNK, SPAN):
            for start in range(0, GROUP * ROWS, TILE):
                attend(start, TILE, block[0, j:j + SPAN, :], block[1, j:j + SPAN, :])

    causal = (
        lax.broadcasted_iota(jnp.int32, (ROWS, ROWS), 1)
        <= lax.broadcasted_iota(jnp.int32, (ROWS, ROWS), 0)
    )
    for h in range(GROUP):
        attend(h * ROWS, ROWS, home[0, CHUNK:, :], home[1, CHUNK:, :], causal)
    absorb(home)

    def step(i, _):
        @pl.when(i == 0)
        def _():
            arrived("own_a_across")
            start("across_a_up", "across_a_down")
            arrived("own_a_up", "own_a_down")
            start(("sibling", NEAR_A))
            arrived(("sibling", OWN))

        @pl.when(i == 1)
        def _():
            arrived("own_b_across")
            start(("sibling", ACROSS))
            arrived(("sibling", NEAR_A))

        @pl.when(i == 2)
        def _():
            arrived("own_b_up", "own_b_down")
            start("up_b_across", "down_b_across", "far_b", "far_a", ("sibling", NEAR_B))
            arrived(("sibling", ACROSS))

        @pl.when(i == 3)
        def _():
            arrived("across_a_up", "across_a_down")
            start("far_across_up", "far_across_down", ("sibling", ACROSS_A))
            arrived(("sibling", NEAR_B))

        @pl.when(i == 4)
        def _():
            arrived("far_b")
            start("far_b_across")
            arrived("far_a")
            start(("sibling", FAR))
            arrived(("sibling", ACROSS_A))

        @pl.when(i == 5)
        def _():
            arrived("up_b_across", "down_b_across")
            start(("sibling", ACROSS_B))
            arrived(("sibling", FAR))

        @pl.when(i == 6)
        def _():
            arrived("far_across_up", "far_across_down", "far_b_across")
            start(("sibling", FAR_ACROSS))
            arrived(("sibling", ACROSS_B))

        absorb(kv.at[2 * i])
        absorb(kv.at[2 * i + 1])
        return 0

    lax.fori_loop(0, 7, step, 0)

    arrived(("sibling", FAR_ACROSS))
    absorb(kv.at[14])
    live = lax.broadcasted_iota(jnp.int32, (ROWS, HEAD), 0) < length[0]
    for h in range(GROUP):
        rows = pl.ds(h * ROWS, ROWS)
        result = acc[rows, 0:HEAD] / acc[rows, HEAD:2 * HEAD]
        out[:, h * HEAD:(h + 1) * HEAD] = jnp.where(live, result, 0.0).astype(BF16)

    for d in range(1, TP):
        a_copy(d).wait_send()
    for copy in moves.values():
        copy.wait_send()


def shards(tokens, norm_gain, query_weight, key_matrix, value_matrix, prompt_cache, lengths):
    cache = prompt_cache.reshape(2 * PIECE * TP, HEAD)
    gain = norm_gain.reshape(PARTS, 1, PART)
    cosine, sine = tables()
    hbm = pl.BlockSpec(memory_space=pl.ANY)
    vmem = pl.BlockSpec(memory_space=pltpu.VMEM)
    smem = pl.BlockSpec(memory_space=pltpu.SMEM)
    return pl.pallas_call(
        kernel,
        out_shape=jax.ShapeDtypeStruct((ROWS, GROUP * HEAD), BF16),
        in_specs=[hbm, vmem, hbm, hbm, hbm, hbm, smem, vmem, vmem],
        out_specs=vmem,
        scratch_shapes=[
            pltpu.VMEM((PARTS, ROWS, PART), BF16),
            pltpu.VMEM((PARTS, ROWS, PART), BF16),
            pltpu.VMEM((PARTS, PART, GROUP * HEAD), BF16),
            pltpu.VMEM((PARTS, PART, HEAD), BF16),
            pltpu.VMEM((PARTS, PART, HEAD), BF16),
            pltpu.VMEM((ROWS, (GROUP + 2) * HEAD), F32),
            pltpu.VMEM((2 * PIECE * TP, HEAD), BF16),
            pltpu.VMEM((2 * PIECE * TP, HEAD), F32),
            pltpu.VMEM((TP, 2, PIECE, HEAD), BF16),
            pltpu.VMEM((2, CHUNK + ROWS, HEAD), BF16),
            pltpu.VMEM((ROLLOUT - 1, 2, CHUNK, HEAD), BF16),
            pltpu.VMEM((GROUP * ROWS, HEAD), BF16),
            pltpu.VMEM((GROUP * ROWS, 128), F32),
            pltpu.VMEM((GROUP * ROWS, 2 * HEAD), F32),
            pltpu.SemaphoreType.DMA((PARTS,)),
            pltpu.SemaphoreType.DMA((3, PARTS)),
            pltpu.SemaphoreType.DMA,
            pltpu.SemaphoreType.DMA((TP - 1,)),
            pltpu.SemaphoreType.DMA((TP - 1,)),
            pltpu.SemaphoreType.DMA((23,)),
            pltpu.SemaphoreType.DMA((23,)),
        ],
        compiler_params=pltpu.CompilerParams(
            collective_id=0, has_side_effects=True, vmem_limit_bytes=62 << 20
        ),
        cost_estimate=pl.CostEstimate(
            flops=23_000_000_000, bytes_accessed=30_000_000, transcendentals=34_000_000
        ),
    )(
        tokens, gain, query_weight, key_matrix, value_matrix, cache, lengths,
        jnp.asarray(cosine), jnp.asarray(sine),
    )


def solution(mesh):
    placed = (
        P("rollout", None),
        P(),
        P(None, "tp"),
        P(None, "tp"),
        P(None, "tp"),
        P(None, ("rollout", "tp"), None, None),
        P("rollout"),
    )
    return jax.shard_map(
        shards, mesh=mesh, in_specs=placed, out_specs=P("rollout", "tp"), check_vma=False
    )
```

time: 76.4 us -> 67.2 us (0.88)
  Pallas kernels: 71.7 us -> 64.4 us
  local copies, waits for them, and re-layouts: 3.81 us -> 1.87 us
    pallas_call x1, Pallas kernels: 71.7 us -> 64.4 us  [shards(): pl.pallas_call(kernel, out_shape=jax.ShapeDtypeStruct((ROWS, GROUP * HEAD...]
    unnamed x2 -> x1, local copies, waits for them, and re-layouts: 3.81 us -> 1.87 us
where the time goes in v2:
time: 67.2 us; the launch traced here: 67 us
  Pallas kernels  64.4 us (96%)
  local copies, waits for them, and re-layouts  1.87 us (3%)
    pallas_call x1, Pallas kernels, shards(): pl.pallas_call(kernel, out_shape=jax.ShapeDtypeStruct((ROWS, GROUP * HEAD...  64.4 us
    unnamed x1, local copies, waits for them, and re-layouts  1.87 us

profile of v2, /device:TPU:0, one launch (start us, length us, event | category | flops | bytes accessed | tf_op | source)
XLA Modules:
  0.0 67.0 jit_solution(4748794522918055003)
XLA Ops:
  0.7 64.4 %shard_map.91 = bf16[256,1024]{1,0:T(8,128)(2,1)} custom-call(bf16[256,8192]{1,0:T(8,128)(2,1)} %tokens.1, f32[8,1,1024]{2,1,0:T(1,128)} %bitcast.3, bf16[8192,1024]{1,0:T(8,128)(2,1)} %wq.1, bf16[8192,128]{1,0:T(8,128)(2,1)} %wk.1, bf16[8192,128]{1,0:T(8,128)(2,1)} %wv.1, bf16[2048,128]{1,0:T(8,128)(2,1)} %bitcast.2, s32[1]{0:T(128)S(6)} %copy.11.length, ...), custom_call_target="tpu_custom_call" | custom-call | flops 23000000512 | bytes 30000000 | tf_op jit(solution)/shard_map/pallas_call | solution.py:346
  65.1 1.9 %copy.12 = bf16[256,1024]{1,0:T(8,128)(2,1)} copy(bf16[256,1024]{1,0:T(8,128)(2,1)} %shard_map.91) | data formatting | bytes 1048576

commit v3 on v2

--- a/solution.py
+++ b/solution.py
@@ -48,7 +48,7 @@
 
 
 def kernel(
-    tokens, gain, wq, wk, wv, cache, length, cos_ref, sin_ref, out,
+    tokens, gain, wq, wk, wv, cache, cos_ref, sin_ref, out,
     tok, normed, wq_v, wk_v, wv_v, proj, raw, wide, by_head, home, kv, q, top, acc,
     tok_sem, w_sem, raw_sem, a_send, a_recv, send, recv,
 ):
@@ -208,7 +208,7 @@
             for (a, b), piece in zip(spans, pieces):
                 proj[:, a:b] += piece
 
-        @pl.when(i == PARTS - 1)
+        @pl.when(i == PARTS - 2)
         def _():
             for d in range(1, 4):
                 a_copy(d).wait_recv()
@@ -324,11 +324,10 @@
 
     arrived(("sibling", FAR_ACROSS))
     absorb(kv.at[14])
-    live = lax.broadcasted_iota(jnp.int32, (ROWS, HEAD), 0) < length[0]
     for h in range(GROUP):
         rows = pl.ds(h * ROWS, ROWS)
         result = acc[rows, 0:HEAD] / acc[rows, HEAD:2 * HEAD]
-        out[:, h * HEAD:(h + 1) * HEAD] = jnp.where(live, result, 0.0).astype(BF16)
+        out[:, h * HEAD:(h + 1) * HEAD] = result.astype(BF16)
 
     for d in range(1, TP):
         a_copy(d).wait_send()
@@ -342,11 +341,10 @@
     cosine, sine = tables()
     hbm = pl.BlockSpec(memory_space=pl.ANY)
     vmem = pl.BlockSpec(memory_space=pltpu.VMEM)
-    smem = pl.BlockSpec(memory_space=pltpu.SMEM)
-    return pl.pallas_call(
+    context = pl.pallas_call(
         kernel,
         out_shape=jax.ShapeDtypeStruct((ROWS, GROUP * HEAD), BF16),
-        in_specs=[hbm, vmem, hbm, hbm, hbm, hbm, smem, vmem, vmem],
+        in_specs=[hbm, vmem, hbm, hbm, hbm, hbm, vmem, vmem],
         out_specs=vmem,
         scratch_shapes=[
             pltpu.VMEM((PARTS, ROWS, PART), BF16),
@@ -378,9 +376,11 @@
             flops=23_000_000_000, bytes_accessed=30_000_000, transcendentals=34_000_000
         ),
     )(
-        tokens, gain, query_weight, key_matrix, value_matrix, cache, lengths,
+        tokens, gain, query_weight, key_matrix, value_matrix, cache,
         jnp.asarray(cosine), jnp.asarray(sine),
     )
+    live = jnp.arange(ROWS)[:, None] < lengths[0]
+    return jnp.where(live, context, jnp.zeros_like(context))
 
 
 def solution(mesh):

time: 67.2 us -> 67.3 us (level); the launches traced: 67 us -> 66.1 us
  other arithmetic: 0 us -> 1.95 us
  local copies, waits for them, and re-layouts: 1.87 us -> 0 us
  Pallas kernels: 64.4 us -> 63.5 us
    select_n x0 -> x1, other arithmetic: none -> 1.94 us  [shards(): return jnp.where(live, context, jnp.zeros_like(context))]
    unnamed x1 -> x0, local copies, waits for them, and re-layouts: 1.87 us -> none
    pallas_call x1, Pallas kernels: 64.4 us -> 63.5 us  [shards(): pl.pallas_call(kernel, out_shape=jax.ShapeDtypeStruct((ROWS, GROUP * HEAD...]
where the time goes in v3:
time: 67.3 us; the launch traced here: 66.1 us
  Pallas kernels  63.5 us (94%)
  other arithmetic  1.95 us (3%)
    pallas_call x1, Pallas kernels, shards(): pl.pallas_call(kernel, out_shape=jax.ShapeDtypeStruct((ROWS, GROUP * HEAD...  63.5 us
    select_n x1, other arithmetic, shards(): return jnp.where(live, context, jnp.zeros_like(context))  1.94 us

profile of v3, /device:TPU:0, one launch (start us, length us, event | category | flops | bytes accessed | tf_op | source)
XLA Modules:
  0.0 66.1 jit_solution(17152301211957207497)
XLA Ops:
  0.7 63.5 %shard_map.91 = bf16[256,1024]{1,0:T(8,128)(2,1)} custom-call(bf16[256,8192]{1,0:T(8,128)(2,1)} %tokens.1, f32[8,1,1024]{2,1,0:T(1,128)} %bitcast.5, bf16[8192,1024]{1,0:T(8,128)(2,1)} %wq.1, bf16[8192,128]{1,0:T(8,128)(2,1)} %wk.1, bf16[8192,128]{1,0:T(8,128)(2,1)} %wv.1, bf16[2048,128]{1,0:T(8,128)(2,1)} %bitcast.4, f32[256,128]{1,0:T(8,128)} %constant.6.clone.cos_ref, ...), custom_call_target="tpu_custom_call" | custom-call | flops 23000000512 | bytes 30000000 | tf_op jit(solution)/shard_map/pallas_call | solution.py:344
  64.2 1.9 %broadcast_select_fusion = bf16[256,1024]{1,0:T(8,128)(2,1)} fusion(bf16[256,1024]{1,0:T(8,128)(2,1)} %shard_map.91, pred[256]{0:T(512)(128)(4,1)S(1)} %iota_compare_fusion), kind=kLoop, calls=%fused_computation | loop fusion | flops 262144 | bytes 1048832 | tf_op jit(solution)/shard_map/jit(_where)/select_n | solution.py:383
  (1 shorter events, 0.0 us)

commit v4 on v3

--- a/solution.py
+++ b/solution.py
@@ -24,7 +24,7 @@
 SCALE = float(HEAD ** -0.5 * np.log2(np.e))
 
 HALF = CHUNK // 2
-EARLY = 4
+EARLY = 6
 TILE = 2048
 SPAN = 256
 OFFSETS = ((0, 0), (0, 1), (1, 0), (3, 0), (1, 1), (3, 1), (2, 0), (2, 1))
@@ -48,9 +48,9 @@
 
 
 def kernel(
-    tokens, gain, wq, wk, wv, cache, cos_ref, sin_ref, out,
-    tok, normed, wq_v, wk_v, wv_v, proj, raw, wide, by_head, home, kv, q, top, acc,
-    tok_sem, w_sem, raw_sem, a_send, a_recv, send, recv,
+    tokens, gain_h, wq, wk, wv, cache, cos_h, sin_h, out,
+    gain, cos_ref, sin_ref, tok, normed, wq_v, wk_v, wv_v, proj, raw, wide, by_head, home, kv, q, top, acc,
+    small_sem, tok_sem, w_sem, raw_sem, a_send, a_recv, send, recv,
 ):
     r, t = lax.axis_index("rollout"), lax.axis_index("tp")
     y, low = r // 4, r % 4
@@ -97,6 +97,13 @@
         return 0
 
     lax.fori_loop(0, PARTS, start_loads, 0)
+    small = [
+        pltpu.make_async_copy(gain_h, gain, small_sem.at[0]),
+        pltpu.make_async_copy(cos_h, cos_ref, small_sem.at[1]),
+        pltpu.make_async_copy(sin_h, sin_ref, small_sem.at[2]),
+    ]
+    for c in small:
+        c.start()
     lax.fori_loop(0, EARLY, start_weights, 0)
 
     raw_copy.wait()
@@ -179,6 +186,8 @@
         normed[i] = (tok[i].astype(F32) * factor * gain[i]).astype(BF16)
         return 0
 
+    for c in small:
+        c.wait()
     lax.fori_loop(0, PARTS, scale, 0)
 
     pl.semaphore_wait(barrier, TP - 1 + 4)
@@ -344,9 +353,12 @@
     context = pl.pallas_call(
         kernel,
         out_shape=jax.ShapeDtypeStruct((ROWS, GROUP * HEAD), BF16),
-        in_specs=[hbm, vmem, hbm, hbm, hbm, hbm, vmem, vmem],
+        in_specs=[hbm] * 8,
         out_specs=vmem,
         scratch_shapes=[
+            pltpu.VMEM((PARTS, 1, PART), F32),
+            pltpu.VMEM((ROWS, HEAD), F32),
+            pltpu.VMEM((ROWS, HEAD), F32),
             pltpu.VMEM((PARTS, ROWS, PART), BF16),
             pltpu.VMEM((PARTS, ROWS, PART), BF16),
             pltpu.VMEM((PARTS, PART, GROUP * HEAD), BF16),
@@ -361,6 +373,7 @@
             pltpu.VMEM((GROUP * ROWS, HEAD), BF16),
             pltpu.VMEM((GROUP * ROWS, 128), F32),
             pltpu.VMEM((GROUP * ROWS, 2 * HEAD), F32),
+            pltpu.SemaphoreType.DMA((3,)),
             pltpu.SemaphoreType.DMA((PARTS,)),
             pltpu.SemaphoreType.DMA((3, PARTS)),
             pltpu.SemaphoreType.DMA,

time: 67.3 us -> 66.4 us (0.987)
  Pallas kernels: 63.5 us -> 62.7 us
    pallas_call x1, Pallas kernels: 63.5 us -> 62.7 us  [shards(): pl.pallas_call(kernel, out_shape=jax.ShapeDtypeStruct((ROWS, GROUP * HEAD...]
where the time goes in v4:
time: 66.4 us; the launch traced here: 65.3 us
  Pallas kernels  62.7 us (94%)
  other arithmetic  1.95 us (3%)
  between operations  0.67 us (1%)
    pallas_call x1, Pallas kernels, shards(): pl.pallas_call(kernel, out_shape=jax.ShapeDtypeStruct((ROWS, GROUP * HEAD...  62.7 us
    select_n x1, other arithmetic, shards(): return jnp.where(live, context, jnp.zeros_like(context))  1.94 us

profile of v4, /device:TPU:0, one launch (start us, length us, event | category | flops | bytes accessed | tf_op | source)
XLA Modules:
  0.0 65.3 jit_solution(6003795998046714002)
XLA Ops:
  0.7 62.7 %shard_map.91 = bf16[256,1024]{1,0:T(8,128)(2,1)} custom-call(bf16[256,8192]{1,0:T(8,128)(2,1)} %tokens.1, f32[8,1,1024]{2,1,0:T(1,128)} %bitcast.5, bf16[8192,1024]{1,0:T(8,128)(2,1)} %wq.1, bf16[8192,128]{1,0:T(8,128)(2,1)} %wk.1, bf16[8192,128]{1,0:T(8,128)(2,1)} %wv.1, bf16[2048,128]{1,0:T(8,128)(2,1)} %bitcast.4, f32[256,128]{1,0:T(8,128)} %constant.6.clone.cos_h, ...), custom_call_target="tpu_custom_call" | custom-call | flops 23000000512 | bytes 30000000 | tf_op jit(solution)/shard_map/pallas_call | solution.py:353
  63.3 1.9 %broadcast_select_fusion = bf16[256,1024]{1,0:T(8,128)(2,1)} fusion(bf16[256,1024]{1,0:T(8,128)(2,1)} %shard_map.91, pred[256]{0:T(512)(128)(4,1)S(1)} %iota_compare_fusion), kind=kLoop, calls=%fused_computation | loop fusion | flops 262144 | bytes 1048832 | tf_op jit(solution)/shard_map/jit(_where)/select_n | solution.py:396
  (1 shorter events, 0.0 us)

commit v5 on v4

--- a/solution.py
+++ b/solution.py
@@ -186,15 +186,16 @@
         normed[i] = (tok[i].astype(F32) * factor * gain[i]).astype(BF16)
         return 0
 
-    for c in small:
-        c.wait()
-    lax.fori_loop(0, PARTS, scale, 0)
-
     pl.semaphore_wait(barrier, TP - 1 + 4)
     for d in range(1, TP):
         a_copy(d).start()
     lax.fori_loop(EARLY, PARTS, start_weights, 0)
     home[:, 0:PIECE, :] = by_head[t]
+
+    for c in small:
+        c.wait()
+    lax.fori_loop(0, PARTS, scale, 0)
+
 
     def project(i, _):
         for c in w_copies(i):

time: 66.4 us -> 66.1 us (level); the launches traced: 65.3 us -> 65.9 us
  no operation moved by 1% of the time
where the time goes in v5:
time: 66.1 us; the launch traced here: 65.9 us
  Pallas kernels  63.3 us (96%)
  other arithmetic  1.95 us (3%)
  between operations  0.67 us (1%)
    pallas_call x1, Pallas kernels, shards(): pl.pallas_call(kernel, out_shape=jax.ShapeDtypeStruct((ROWS, GROUP * HEAD...  63.3 us
    select_n x1, other arithmetic, shards(): return jnp.where(live, context, jnp.zeros_like(context))  1.94 us

profile of v5, /device:TPU:0, one launch (start us, length us, event | category | flops | bytes accessed | tf_op | source)
XLA Modules:
  0.0 65.9 jit_solution(2003002909570719243)
XLA Ops:
  0.7 63.3 %shard_map.91 = bf16[256,1024]{1,0:T(8,128)(2,1)} custom-call(bf16[256,8192]{1,0:T(8,128)(2,1)} %tokens.1, f32[8,1,1024]{2,1,0:T(1,128)} %bitcast.5, bf16[8192,1024]{1,0:T(8,128)(2,1)} %wq.1, bf16[8192,128]{1,0:T(8,128)(2,1)} %wk.1, bf16[8192,128]{1,0:T(8,128)(2,1)} %wv.1, bf16[2048,128]{1,0:T(8,128)(2,1)} %bitcast.4, f32[256,128]{1,0:T(8,128)} %constant.6.clone.cos_h, ...), custom_call_target="tpu_custom_call" | custom-call | flops 23000000512 | bytes 30000000 | tf_op jit(solution)/shard_map/pallas_call | solution.py:354
  64.0 1.9 %broadcast_select_fusion = bf16[256,1024]{1,0:T(8,128)(2,1)} fusion(bf16[256,1024]{1,0:T(8,128)(2,1)} %shard_map.91, pred[256]{0:T(512)(128)(4,1)S(1)} %iota_compare_fusion), kind=kLoop, calls=%fused_computation | loop fusion | flops 262144 | bytes 1048832 | tf_op jit(solution)/shard_map/jit(_where)/select_n | solution.py:397
  (1 shorter events, 0.0 us)
